TPU v7x, 256 devices: a whole 4x4x8 slice. The times are simulated.
256 devices in a mesh: row: 8 (over y, core), blk: 32 (over x, z).
Axes of the slice: x: 4, y: 4, z: 8, core: 2. Of those that a mesh axis runs over, the one named last changes fastest.
Arguments:
- theta: float32 [32, 32, 256, 256], P('blk'), may hold values from -6 to 6
- left_env: float32 [16, 32, 256, 256], P('row', 'blk'), may hold values from -0.375 to 0.375
- right_env: float32 [16, 32, 256, 256], P('row', 'blk'), may hold values from -0.375 to 0.375
- left_tiles: int32 [32], replicated, may hold values from 1 to 4
- right_tiles: int32 [32], replicated, may hold values from 1 to 4
- pairs: int32 [48, 2], replicated, may hold values from 0 to 15
- coefs: float32 [48], replicated, may hold values from -2 to 2
Outputs:
- hpsi: float32 [32, 32, 256, 256], P('blk', None, 'row')
All inputs are finite; a program needn't handle non-finite values.
Results may differ from a plain program's by a relative error of at most 0.000071.
Values sent between devices are 32-bit elements; how exact they have to be, the bound alone decides.
A program may use at most 128 MiB of HBM per device.

v0:
```python
import jax
import jax.numpy as jnp
from jax import lax
from jax.sharding import PartitionSpec as P


def per_device(theta, left_env, right_env, left_tiles, right_tiles, pairs, coefs):
    bond_local = left_env.shape[0]
    bond_total = bond_local * lax.axis_size("row")
    left_count = theta.shape[0]
    block_rows = theta.shape[2]
    row_parts = lax.axis_size("row")
    row_at = lax.axis_index("row")
    blk_at = lax.axis_index("blk")
    quarter = block_rows // 4
    cells = jnp.arange(block_rows)
    tiles_here = lax.dynamic_slice_in_dim(left_tiles, blk_at * left_count, left_count, 0)
    left_mask = (cells[None, :] < quarter * tiles_here[:, None]).astype(jnp.float32)
    right_mask = (cells[None, :] < quarter * right_tiles[:, None]).astype(jnp.float32)
    masked = theta * left_mask[:, None, :, None] * right_mask[None, :, None, :]
    bonds = jnp.arange(bond_total)
    onehot_left = (pairs[:, 0][:, None] == bonds[None, :]).astype(jnp.float32)
    onehot_right = (pairs[:, 1][:, None] == bonds[None, :]).astype(jnp.float32)
    couplings = jnp.einsum(
        "ka,kb->ab", onehot_left * coefs[:, None], onehot_right, precision=lax.Precision.HIGHEST
    )
    couple_local = lax.dynamic_slice_in_dim(couplings, row_at * bond_local, bond_local, 1)
    dressed = lax.psum_scatter(
        jnp.einsum("ab,bqij->aqij", couple_local, right_env, precision=lax.Precision.HIGHEST),
        "row",
        scatter_dimension=0,
        tiled=True,
    )
    slab = block_rows // row_parts
    row_ids = row_at * slab + jnp.arange(slab)
    out_left = (row_ids[None, :] < quarter * tiles_here[:, None]).astype(jnp.float32)
    partial_value = jnp.einsum(
        "apij,pqjk->apqik", left_env, masked, precision=lax.Precision.HIGHEST
    )
    summed = jnp.einsum(
        "apqik,aqlk->pqil",
        partial_value,
        lax.all_gather(dressed, "blk", axis=1, tiled=True),
        precision=lax.Precision.HIGHEST,
    )
    result = lax.psum_scatter(summed, "row", scatter_dimension=2, tiled=True)
    return result * out_left[:, None, :, None] * right_mask[None, :, None, :]


def solution(mesh):
    return jax.shard_map(
        per_device,
        mesh=mesh,
        in_specs=(
            P("blk", None, None, None),
            P("row", "blk", None, None),
            P("row", "blk", None, None),
            P(),
            P(),
            P(),
            P(),
        ),
        out_specs=P("blk", None, "row", None),
        check_vma=False,
    )
```

profile of v0, /device:TPU:1, one launch (start us, length us, event | category | flops | bytes accessed | tf_op | source)
XLA Modules:
  0.0 299.0 jit_solution(14616747407811944352)
XLA Ops:
  6.5 0.0 copy-start
  6.5 0.0 reduce-scatter.3.cloned.1.call-start
  6.5 0.8 slice_bitcast_fusion.1
  7.3 0.9 fusion.14
  8.2 0.0 copy-start.2
  8.2 0.0 copy-start.3
  8.2 4.8 %convolution_bitcast_fusion = f32[16,1,256,256]{3,0,2,1:T(8,128)S(1)} fusion(f32[2,256,256]{2,1,0:T(8,128)} %bitcast.40, f32[16,16]{0,1:T(8,128)S(1)} %fusion.14, s32[]{:T(128)S(6)} %select_n.6), kind=kOutput, calls=%fused_computation.9 | convolution fusion | flops 25165824 | bytes 4719620 | tf_op jit(solution)/shard_map/ab,bqij->aqij/dot_general | solution.py:29
  13.0 4.4 %copy.14 = f32[16,1,256,256]{3,2,1,0:T(8,128)} copy(f32[16,1,256,256]{3,0,2,1:T(8,128)S(1)} %convolution_bitcast_fusion) | data formatting | bytes 8388608 | tf_op jit(solution)/shard_map/ab,bqij->aqij/dot_general | solution.py:29
  17.4 0.0 reduce-scatter.3.cloned.1.call-update
  17.4 0.0 all-gather.2.cloned.1.call-start
  17.5 41.4 %reduce-scatter.3.cloned.1.call-done = f32[2,1,256,256]{3,2,1,0:T(8,128)} async-done(((f32[16,1,256,256]{3,2,1,0:T(8,128)}), f32[2,1,256,256]{3,2,1,0:T(8,128)}) %reduce-scatter.3.cloned.1.call-update) | async-done | bytes 524304 | tf_op jit(solution)/shard_map/reduce_scatter | solution.py:28
  58.9 0.0 all-gather.2.cloned.1.call-update
  58.9 0.2 reduce-scatter.5.cloned.1.call-start
  59.1 0.0 copy-done.2
  59.1 0.6 dynamic_slice.7
  60.4 0.0 copy-done.3
  60.4 0.1 fusion.13
  60.5 0.0 copy-done
  60.5 31.7 %fusion.2 = f32[32,256,2,256]{3,1,2,0:T(8,128)} fusion(f32[1,32,256,256]{3,2,1,0:T(8,128)} %param.7, f32[32,256]{1,0:T(8,128)S(1)} %fusion.13, f32[256]{0:T(256)S(1)} %compare_convert_fusion.1, f32[2,1,256,256]{3,2,1,0:T(8,128)S(1)} %copy-done), kind=kOutput, calls=%fused_computation.2 | convolution fusion | flops 12889096192 | bytes 25723904 | tf_op jit(solution)/shard_map/apij,pqjk->apqik/dot_general | solution.py:37
  92.2 111.2 %all-gather.2.cloned.1.call-done = f32[2,32,256,256]{3,2,0,1:T(8,128)} async-done(((f32[2,1,256,256]{3,2,0,1:T(8,128)}), f32[2,32,256,256]{3,2,0,1:T(8,128)}) %all-gather.2.cloned.1.call-update) | async-done | bytes 16777232 | tf_op jit(solution)/shard_map/all_gather | solution.py:43
  203.4 23.7 %fusion.8 = f32[1,32,256,256]{2,3,1,0:T(8,128)} fusion(f32[2,32,256,256]{3,2,0,1:T(8,128)} %all-gather.2.cloned.1.call-done, f32[32,256,2,256]{3,1,2,0:T(8,128)} %fusion.2), kind=kOutput, calls=%fused_computation.8 | convolution fusion | flops 12884901888 | bytes 41943040 | tf_op jit(solution)/shard_map/apqik,aqlk->pqil/dot_general | solution.py:40
  227.1 0.0 copy-start.1
  227.1 10.3 %copy.18 = f32[1,32,256,256]{3,1,0,2:T(8,128)} copy(f32[1,32,256,256]{2,3,1,0:T(8,128)} %fusion.8) | data formatting | bytes 16777216 | tf_op jit(solution)/shard_map/apqik,aqlk->pqil/transpose | solution.py:40
  237.5 0.0 reduce-scatter.5.cloned.1.call-update
  237.5 52.0 %reduce-scatter.5.cloned.1.call-done = f32[1,32,32,256]{3,1,0,2:T(8,128)} async-done(((f32[1,32,256,256]{3,1,0,2:T(8,128)}), f32[1,32,32,256]{3,1,0,2:T(8,128)}) %reduce-scatter.5.cloned.1.call-update) | async-done | bytes 1048592 | tf_op jit(solution)/shard_map/reduce_scatter | solution.py:46
  289.5 1.4 multiply_multiply_fusion
  290.9 1.6 copy.19
  292.5 0.0 copy-done.1
  (3 shorter events, 0.0 us)
Async XLA Ops:
  6.5 53.9 %copy-start = (f32[2,1,256,256]{3,2,1,0:T(8,128)S(1)}, f32[2,1,256,256]{3,2,1,0:T(8,128)}, u32[]{:S(2)}) copy-start(f32[2,1,256,256]{3,2,1,0:T(8,128)} %param.8) | copy-start | bytes 1572868
  6.5 52.3 %reduce-scatter.3.cloned.1.call-start = ((), (), s32[]{:S(2)}) async-start(), calls=%async_computation.2 | async-start | bytes 4718592 | tf_op jit(solution)/shard_map/reduce_scatter | solution.py:28
  8.2 50.9 %copy-start.2 = (s32[32]{0:T(128)S(1)}, s32[32]{0:T(128)}, u32[]{:S(2)}) copy-start(s32[32]{0:T(128)} %param.10) | copy-start | bytes 388
  8.2 52.2 %copy-start.3 = (s32[32]{0:T(128)S(1)}, s32[32]{0:T(128)}, u32[]{:S(2)}) copy-start(s32[32]{0:T(128)} %param.11) | copy-start | bytes 388
  17.4 186.0 %all-gather.2.cloned.1.call-start = ((), (), s32[]{:S(2)}) async-start(), calls=%async_computation.3 | async-start | bytes 17301504 | tf_op jit(solution)/shard_map/all_gather | solution.py:43
  58.9 230.6 %reduce-scatter.5.cloned.1.call-start = ((), (), s32[]{:S(2)}) async-start(), calls=%async_computation.4 | async-start | bytes 9437184 | tf_op jit(solution)/shard_map/reduce_scatter | solution.py:46
  227.1 65.4 %copy-start.1 = (f32[2,1,256,256]{3,2,1,0:T(8,128)S(1)}, f32[2,1,256,256]{3,2,1,0:T(8,128)}, u32[]{:S(2)}) copy-start(f32[2,1,256,256]{3,2,1,0:T(8,128)} %param.8) | copy-start | bytes 1572868
Sparse Core Ops, SparseCore 0:
  17.6 41.2 reduce-scatter.2
  61.5 141.9 all-gather.1
  237.6 51.8 reduce-scatter.4
where the time goes:
time: 299 us
  waiting for transfers between devices  205 us (69%)
  matrix products  61.1 us (20%)
  local copies, waits for them, and re-layouts  17.7 us (6%)
  between operations  13.8 us (5%)
    all_gather x1, waiting for transfers between devices, per_device(): lax.all_gather(dressed, 'blk', axis=1, tiled=True)  111 us
    reduce_scatter x1, waiting for transfers between devices, per_device(): result = lax.psum_scatter(summed, 'row', scatter_dimension=2, tiled=True)  52 us
    reduce_scatter x1, waiting for transfers between devices, per_device(): lax.psum_scatter(jnp.einsum('ab,bqij->aqij', couple_local, right_env, pre...  41.4 us
    dot_general x1, matrix products, per_device(): jnp.einsum('apij,pqjk->apqik', left_env, masked, precision=lax.Precision....  31.7 us
    dot_general x1, matrix products, per_device(): jnp.einsum('apqik,aqlk->pqil', partial_value, lax.all_gather(dressed, 'bl...  23.7 us
    transpose x1, local copies, waits for them, and re-layouts, per_device(): jnp.einsum('apqik,aqlk->pqil', partial_value, lax.all_gather(dressed, 'bl...  10.3 us
  transfers between devices with their start and end apart: 3, of which 3 were waited for; matrix products, arithmetic and copies ran while one was open for 11% of the time, Pallas kernels for 0%

commit v1 on v0

v1 whole, which is shorter than its diff:
```python
import functools

import jax
import jax.numpy as jnp
from jax import lax
from jax.experimental import pallas as pl
from jax.experimental.pallas import tpu as pltpu
from jax.sharding import PartitionSpec as P

MESH = pl.DeviceIdType.MESH
F32 = jnp.float32
BF16 = jnp.bfloat16
NX, NY, NZ = 4, 4, 8
MB = 256
SLAB = 32
DIST = (0, 1, 7, 2, 6, 3, 5, 4)
POS = tuple(DIST.index(d) for d in range(8))
GROUPS = ((0, 0), (1, 0), (3, 0), (2, 0), (0, 1), (1, 1), (3, 1), (2, 1))
NG = len(GROUPS)


def pick(table, at):
    return sum((at == i).astype(jnp.int32) * v for i, v in enumerate(table) if v)


def split(v):
    hi = v.astype(BF16)
    return hi, (v - hi.astype(F32)).astype(BF16)


def dot(a, b):
    return jnp.dot(a, b, preferred_element_type=F32)


def kernel(
    coup, lt, rt, th_in, l_in, r_in, o_ref,
    th, rin, rbuf, rhi, rlo, lall, xbuf, xhi, xlo, part, sib, f1, f2, fin,
    loc, own_s, l_s, l_r, z_s, z_r, t_s, t_r, ts_s, ts_r, q_s, q_r, x_s, x_r,
    p_s, p_r, f1_s, f1_r, f2_s, f2_r, o_s, o_r, o_l,
):
    row, blk = lax.axis_index("row"), lax.axis_index("blk")
    y, c = row // 2, row % 2
    x, z = blk // NZ, blk % NZ
    other = 1 - c

    def at(dx=0, dy=0, dz=0, flip=False):
        core = other if flip else c
        return (((y + dy) % NY) * 2 + core, ((x + dx) % NX) * NZ + (z + dz) % NZ)

    yp, ym, y2 = at(dy=1), at(dy=3), at(dy=2)
    xp, xm, x2 = at(dx=1), at(dx=3), at(dx=2)
    zp, zm = at(dz=1), at(dz=7)
    sb = at(flip=True)
    rp, rm, r2 = (row + 2) % 8, (row + 6) % 8, (row + 4) % 8
    srow = y * 2 + other
    sp, sm, s2 = (srow + 2) % 8, (srow + 6) % 8, (srow + 4) % 8

    def rc(src, dst, ss, rs, to):
        return pltpu.make_async_remote_copy(
            src_ref=src, dst_ref=dst, send_sem=ss, recv_sem=rs, device_id=to, device_id_type=MESH
        )

    sends = []
    mine = [2 * k + c for k in range(4)]
    theirs = [2 * k + other for k in range(4)]

    def view(of):
        return of[0].at[of[1]]

    def send(src, dst, ss, rs, to):
        rc(view(src), view(dst), view(ss), view(rs), to).start()
        sends.append((src, ss))

    def got(dst, rs):
        rc(dst, dst, rs, rs, sb).wait_recv()

    def sent(src, ss):
        rc(src, src, ss, ss, sb).wait_send()

    pltpu.make_async_copy(r_in.at[:, 0], rin, loc.at[0]).start()
    pltpu.make_async_copy(l_in.at[:, 0], lall.at[row], loc.at[1]).start()
    for i in range(8):
        pltpu.make_async_copy(
            th_in.at[0, x * NZ + (z + DIST[i]) % NZ], th.at[0, i], own_s.at[i]
        ).start()

    barrier = pltpu.get_barrier_semaphore()
    partners = (yp, ym, xp, xm, x2, zp, zm, sb)
    for t in partners:
        pl.semaphore_signal(barrier, inc=1, device_id=t, device_id_type=MESH)
    pl.semaphore_wait(barrier, len(partners))

    for i, t in enumerate((yp, ym, sb)):
        send((l_in, (slice(None), 0)), (lall, (row,)), (l_s, (i,)), (l_r, (i,)), t)

    def theta_at(xx, i):
        return (th_in, (0, xx * NZ + (z + i) % NZ,))

    def send_theta(k):
        d = DIST[2 * k] + c * (DIST[2 * k + 1] - DIST[2 * k])
        send(theta_at((x + 1) % NX, d), (th, (3, mine[k],)), (t_s, (0, k,)), (t_r, (0, k,)), xp)
        send(theta_at((x + 3) % NX, d), (th, (1, mine[k],)), (t_s, (1, k,)), (t_r, (1, k,)), xm)

    send_theta(0)
    send_theta(1)
    send(theta_at((x + 2) % NX, pick(DIST, row)), (th, (2, row,)), (q_s, (8,)), (q_r, (8,)), x2)

    row_ids = lax.broadcasted_iota(jnp.int32, (MB, MB), 0)
    col_ids = lax.broadcasted_iota(jnp.int32, (MB, MB), 1)
    pltpu.make_async_copy(r_in.at[:, 0], rin, loc.at[0]).wait()
    rlim = (MB // 4) * rt[blk]
    for b in range(2):
        v = jnp.where((row_ids < rlim) & (col_ids < rlim), rin[b], 0.0)
        rbuf[0, b] = v.T

    def z_send(k, b, up):
        if up:
            src, dst = (rbuf, (POS[(8 - k) % 8], b)), (rbuf, (POS[(7 - k) % 8], b))
        else:
            src, dst = (rbuf, (POS[k], b)), (rbuf, (POS[k + 1], b))
        s = 0 if up else 1
        send(src, dst, (z_s, (s, k, b,)), (z_r, (s, k, b,)), zp if up else zm)

    def z_got(k, b, up):
        s = 0 if up else 1
        got(rbuf.at[POS[8 - k] if up else POS[k], b], z_r.at[s, k - 1, b])

    def z_forward(k):
        for b in range(2):
            for up in (True, False):
                z_got(k, b, up)
                if k < 3 or b == (0 if up else 1):
                    z_send(k, b, up)

    for b in range(2):
        z_send(0, b, True)
        z_send(0, b, False)

    def split_r(pos):
        for b in range(2):
            hi, lo = split(rbuf[pos, b])
            rhi[pos, b * MB : (b + 1) * MB, :] = hi
            rlo[pos, b * MB : (b + 1) * MB, :] = lo

    split_r(0)

    got(lall.at[rm], l_r.at[0])
    send((lall, (rm, 0,)), (lall, (rm, 0,)), (l_s, (3,)), (l_r, (3,)), yp)
    send((lall, (rm,)), (lall, (rm,)), (l_s, (5,)), (l_r, (5,)), sb)
    got(lall.at[rp], l_r.at[1])
    send((lall, (rp, 1,)), (lall, (rp, 1,)), (l_s, (4,)), (l_r, (4,)), ym)
    send((lall, (rp,)), (lall, (rp,)), (l_s, (6,)), (l_r, (6,)), sb)

    z_forward(1)

    got(th.at[2, row], q_r.at[8])

    def sib_theta(k):
        for s, dx in ((0, 3), (1, 1)):
            got(th.at[dx, mine[k]], t_r.at[s, k])
            send((th, (dx, mine[k],)), (th, (dx, mine[k],)), (ts_s, (s, k,)), (ts_r, (s, k,)), sb)

    def sib_theta_got(k):
        for s, dx in ((0, 3), (1, 1)):
            got(th.at[dx, theirs[k]], ts_r.at[s, k])

    sib_theta(0)
    sib_theta(1)

    got(lall.at[r2, 0], l_r.at[3])
    got(lall.at[r2, 1], l_r.at[4])
    send((lall, (r2,)), (lall, (r2,)), (l_s, (7,)), (l_r, (7,)), sb)
    for i, t in enumerate((yp, ym, sb)):
        send((th, (2, row,)), (th, (2, row,)), (q_s, (i,)), (q_r, (i,)), t)
    got(lall.at[srow], l_r.at[2])
    got(lall.at[sm], l_r.at[5])
    got(lall.at[sp], l_r.at[6])
    got(lall.at[s2], l_r.at[7])
    pltpu.make_async_copy(l_in.at[:, 0], lall.at[row], loc.at[1]).wait()

    llim = (MB // 4) * lt[blk]
    strip = 32

    @pl.loop(0, MB // strip)
    def _(s):
        first = pl.multiple_of(s * strip, strip)
        rows = lax.broadcasted_iota(jnp.int32, (strip, MB), 0) + first
        cols = lax.broadcasted_iota(jnp.int32, (strip, MB), 1)
        keep = (rows < llim) & (cols < llim)

        def add(r, acc):
            for a in range(2):
                v = lall[r, a, pl.ds(first, strip), :]
                acc = [acc[b] + coup[2 * r + a, 2 * row + b] * v for b in range(2)]
            return acc

        acc = lax.fori_loop(0, 8, add, [jnp.zeros((strip, MB), F32) for _ in range(2)], unroll=True)
        for b in range(2):
            v = jnp.where(keep, acc[b], 0.0)
            xbuf[0, b, pl.ds(first, strip), :] = v
            hi, lo = split(v)
            xhi[0, pl.ds(b * MB + first, strip), :] = hi
            xlo[0, pl.ds(b * MB + first, strip), :] = lo

    for b in range(2):
        send((xbuf, (0, b,)), (xbuf, (3, b,)), (x_s, (0, b,)), (x_r, (0, b,)), xp)
        send((xbuf, (0, b,)), (xbuf, (1, b,)), (x_s, (1, b,)), (x_r, (1, b,)), xm)
    send_theta(2)
    send_theta(3)

    def split_x(dx):
        for b in range(2):
            hi, lo = split(xbuf[dx, b])
            xhi[dx, b * MB : (b + 1) * MB, :] = hi
            xlo[dx, b * MB : (b + 1) * MB, :] = lo

    def event0():
        z_forward(2)
        for i in range(8):
            pltpu.make_async_copy(th_in.at[0, x * NZ + (z + DIST[i]) % NZ], th.at[0, i], own_s.at[i]).wait()
        for pos in (1, 2, 3):
            split_r(pos)
        got(th.at[2, rm], q_r.at[0])
        send((th, (2, rm, pl.ds(0, MB // 2),)), (th, (2, rm, pl.ds(0, MB // 2),)), (q_s, (3,)), (q_r, (3,)), yp)
        send((th, (2, rm,)), (th, (2, rm,)), (q_s, (5,)), (q_r, (5,)), sb)
        got(th.at[2, rp], q_r.at[1])
        send((th, (2, rp, pl.ds(MB // 2, MB // 2),)), (th, (2, rp, pl.ds(MB // 2, MB // 2),)), (q_s, (4,)), (q_r, (4,)), ym)
        send((th, (2, rp,)), (th, (2, rp,)), (q_s, (6,)), (q_r, (6,)), sb)

    def event1():
        got(xbuf.at[3, 0], x_r.at[0, 0])
        send((xbuf, (3, 0,)), (xbuf, (2, 0,)), (x_s, (2, 0,)), (x_r, (2, 0,)), xp)
        got(xbuf.at[1, 0], x_r.at[1, 0])
        got(xbuf.at[1, 1], x_r.at[1, 1])
        send((xbuf, (1, 1,)), (xbuf, (2, 1,)), (x_s, (2, 1,)), (x_r, (2, 1,)), xm)
        split_x(1)
        sib_theta_got(0)
        sib_theta_got(1)

    def event2():
        got(xbuf.at[3, 1], x_r.at[0, 1])
        split_x(3)
        z_forward(3)

    def event3():
        got(th.at[2, r2, pl.ds(0, MB // 2)], q_r.at[3])
        got(th.at[2, r2, pl.ds(MB // 2, MB // 2)], q_r.at[4])
        send((th, (2, r2,)), (th, (2, r2,)), (q_s, (7,)), (q_r, (7,)), sb)
        got(th.at[2, srow], q_r.at[2])
        got(th.at[2, sm], q_r.at[5])
        got(th.at[2, sp], q_r.at[6])
        got(th.at[2, s2], q_r.at[7])
        got(xbuf.at[2, 0], x_r.at[2, 0])
        got(xbuf.at[2, 1], x_r.at[2, 1])
        split_x(2)

    def event4():
        sib_theta(2)
        sib_theta(3)
        z_got(4, 0, True)
        z_got(4, 1, False)
        for pos in (4, 5, 6, 7):
            split_r(pos)

    def event5():
        sib_theta_got(2)
        sib_theta_got(3)

    events = (event0, event1, event2, event3, event4, event5)

    def out_copy(g, j):
        dx, half = pick([a for a, _ in GROUPS], g), pick([h for _, h in GROUPS], g)
        d = pick(DIST, half * 4 + j)
        q = x * NZ + (z + d) % NZ
        return dx, q

    yn, yd, yf = (y + 1) % NY, (y + 3) % NY, (y + 2) % NY

    def stage3(g):
        got(f2.at[g, 0], f2_r.at[g, 0])
        got(f2.at[g, 1], f2_r.at[g, 1])
        fin[g] = part[g, c, y] + f2[g, 0] + f2[g, 1]
        for j in range(4):
            dx, q = out_copy(g, j)

            @pl.when(dx == 0)
            def _():
                pltpu.make_async_copy(fin.at[g, j], o_ref.at[0, q], o_l.at[g, j]).start()

            @pl.when(dx != 0)
            def _():
                to = (row, ((x + dx) % NX) * NZ + z)
                rc(fin.at[g, j], o_ref.at[0, q], o_s.at[g, j], o_r.at[g, j], to).start()

    def stage2(g):
        got(f1.at[g, 0], f1_r.at[g, 0])
        part[g, c, yn, 0:2] = part[g, c, yn, 0:2] + f1[g, 0]
        rc(part.at[g, c, yn], f2.at[g, 0], f2_s.at[g, 0], f2_r.at[g, 0], yp).start()
        got(f1.at[g, 1], f1_r.at[g, 1])
        part[g, c, yd, 2:4] = part[g, c, yd, 2:4] + f1[g, 1]
        rc(part.at[g, c, yd], f2.at[g, 1], f2_s.at[g, 1], f2_r.at[g, 1], ym).start()

    def stage1(g):
        got(sib.at[g], p_r.at[g])
        part[g, c, yf] = part[g, c, yf] + sib[g, yf]
        rc(part.at[g, c, yf, 0:2], f1.at[g, 0], f1_s.at[g, 0], f1_r.at[g, 0], yp).start()
        rc(part.at[g, c, yf, 2:4], f1.at[g, 1], f1_s.at[g, 1], f1_r.at[g, 1], ym).start()
        for yy in (yn, yd, y):
            part[g, c, yy] = part[g, c, yy] + sib[g, yy]

    def compute(g):
        dx, half = pick([a for a, _ in GROUPS], g), pick([h for _, h in GROUPS], g)

        @pl.loop(0, 4)
        def _(j):
            pos = half * 4 + j
            thi, tlo = split(th[dx, pos])
            p = dot(xhi[dx], thi) + dot(xhi[dx], tlo) + dot(xlo[dx], thi)
            wide = jnp.concatenate([p[:MB], p[MB:]], axis=1)
            phi, plo = split(wide)
            o = dot(phi, rhi[pos]) + dot(phi, rlo[pos]) + dot(plo, rhi[pos])
            for s in range(8):
                part[g, s % 2, s // 2, j] = o[s * SLAB : (s + 1) * SLAB, :]

        rc(part.at[g, other], sib.at[g], p_s.at[g], p_r.at[g], sb).start()

    @pl.loop(0, NG + 3)
    def _(g):
        @pl.when(g >= 3)
        def _():
            stage3(g - 3)

        @pl.when((g >= 2) & (g < NG + 2))
        def _():
            stage2(g - 2)

        @pl.when((g >= 1) & (g < NG + 1))
        def _():
            stage1(g - 1)

        for i, event in enumerate(events):
            pl.when(g == i)(event)

        @pl.when(g < NG)
        def _():
            compute(g)

    @pl.loop(0, NG)
    def _(g):
        sent(part.at[g, other], p_s.at[g])
        sent(part.at[g, c, yf, 0:2], f1_s.at[g, 0])
        sent(part.at[g, c, yf, 2:4], f1_s.at[g, 1])
        sent(part.at[g, c, yn], f2_s.at[g, 0])
        sent(part.at[g, c, yd], f2_s.at[g, 1])
        for j in range(4):
            dx, q = out_copy(g, j)
            back = ((x + NX - dx) % NX) * NZ + q % NZ

            @pl.when(dx == 0)
            def _():
                pltpu.make_async_copy(fin.at[g, j], o_ref.at[0, q], o_l.at[g, j]).wait()

            @pl.when(dx != 0)
            def _():
                sent(fin.at[g, j], o_s.at[g, j])
                got(o_ref.at[0, back], o_r.at[g, j])

    for src, ss in sends:
        sent(view(src), view(ss))


def apply(coup, lt, rt, theta, left_env, right_env):
    dma = pltpu.SemaphoreType.DMA
    return pl.pallas_call(
        kernel,
        out_shape=jax.ShapeDtypeStruct((1, NX * NZ, SLAB, MB), F32),
        in_specs=[pl.BlockSpec(memory_space=pltpu.SMEM)] * 3 + [pl.BlockSpec(memory_space=pl.ANY)] * 3,
        out_specs=pl.BlockSpec(memory_space=pl.ANY),
        scratch_shapes=[
            pltpu.VMEM((4, 8, MB, MB), F32),
            pltpu.VMEM((2, MB, MB), F32),
            pltpu.VMEM((8, 2, MB, MB), F32),
            pltpu.VMEM((8, 2 * MB, MB), BF16),
            pltpu.VMEM((8, 2 * MB, MB), BF16),
            pltpu.VMEM((8, 2, MB, MB), F32),
            pltpu.VMEM((4, 2, MB, MB), F32),
            pltpu.VMEM((4, 2 * MB, MB), BF16),
            pltpu.VMEM((4, 2 * MB, MB), BF16),
            pltpu.VMEM((NG, 2, 4, 4, SLAB, MB), F32),
            pltpu.VMEM((NG, 4, 4, SLAB, MB), F32),
            pltpu.VMEM((NG, 2, 2, SLAB, MB), F32),
            pltpu.VMEM((NG, 2, 4, SLAB, MB), F32),
            pltpu.VMEM((NG, 4, SLAB, MB), F32),
            dma((2,)), dma((8,)),
            dma((8,)), dma((8,)),
            dma((2, 4, 2)), dma((2, 4, 2)),
            dma((2, 4)), dma((2, 4)),
            dma((2, 4)), dma((2, 4)),
            dma((9,)), dma((9,)),
            dma((3, 2)), dma((3, 2)),
            dma((NG,)), dma((NG,)),
            dma((NG, 2)), dma((NG, 2)),
            dma((NG, 2)), dma((NG, 2)),
            dma((NG, 4)), dma((NG, 4)), dma((NG, 4)),
        ],
        compiler_params=pltpu.CompilerParams(
            collective_id=0, has_side_effects=True, vmem_limit_bytes=56 * 2**20
        ),
        name="hpsi",
    )(coup, lt, rt, theta, left_env, right_env)


def per_device(theta, left_env, right_env, left_tiles, right_tiles, pairs, coefs):
    bonds = jnp.arange(16)
    onehot_left = (pairs[:, 0][:, None] == bonds[None, :]).astype(F32)
    onehot_right = (pairs[:, 1][:, None] == bonds[None, :]).astype(F32)
    couplings = jnp.einsum(
        "ka,kb->ab", onehot_left * coefs[:, None], onehot_right, precision=lax.Precision.HIGHEST
    )
    return apply(couplings, left_tiles, right_tiles, theta, left_env, right_env)


def solution(mesh):
    return jax.shard_map(
        per_device,
        mesh=mesh,
        in_specs=(
            P("blk", None, None, None),
            P("row", "blk", None, None),
            P("row", "blk", None, None),
            P(),
            P(),
            P(),
            P(),
        ),
        out_specs=P("blk", None, "row", None),
        check_vma=False,
    )
```

time: 299 us -> 112 us (0.37)
  waiting for transfers between devices: 205 us -> 0 us
  Pallas kernels: 0 us -> 106 us
  matrix products: 61.1 us -> 1.52 us
  local copies, waits for them, and re-layouts: 17.7 us -> 3.07 us
  between operations: 13.8 us -> 0.01 us
    all_gather x1 -> x0, waiting for transfers between devices: 111 us -> none  [per_device(): lax.all_gather(dressed, 'blk', axis=1, tiled=True)]
    pallas_call x0 -> x1, Pallas kernels: none -> 106 us  [apply(): pl.pallas_call(kernel, out_shape=jax.ShapeDtypeStruct((1, NX * NZ, SLAB,...]
    reduce_scatter x2 -> x0, waiting for transfers between devices: 93.4 us -> none  [the longest x1 52 us: per_device(): result = lax.psum_scatter(summed, 'row', scatter_dimension=2, tiled=True)]
    dot_general x3 -> x0, matrix products: 60.2 us -> none  [the longest x1 31.7 us: per_device(): jnp.einsum('apij,pqjk->apqik', left_env, masked, precision=lax.Precision....]
    transpose x1 -> x0, local copies, waits for them, and re-layouts: 10.3 us -> none  [per_device(): jnp.einsum('apqik,aqlk->pqil', partial_value, lax.all_gather(dressed, 'bl...]
    dot_general x1 -> x0, local copies, waits for them, and re-layouts: 4.37 us -> none  [per_device(): jnp.einsum('ab,bqij->aqij', couple_local, right_env, precision=lax.Precis...]
  transfers between devices with their start and end apart: 3 -> 0, of which waited for: 3 -> 0; matrix products, arithmetic and copies ran while one was open for 11% -> 0% of each run, Pallas kernels for 0% -> 0%
where the time goes in v1:
time: 112 us; the launch traced here: 110 us
  Pallas kernels  106 us (95%)
  local copies, waits for them, and re-layouts  3.07 us (3%)
  matrix products  1.52 us (1%)
    pallas_call x1, Pallas kernels, apply(): pl.pallas_call(kernel, out_shape=jax.ShapeDtypeStruct((1, NX * NZ, SLAB,...  106 us
    unnamed x1, local copies, waits for them, and re-layouts  2.31 us

profile of v1, /device:TPU:1, one launch (start us, length us, event | category | flops | bytes accessed | tf_op | source)
XLA Modules:
  0.0 110.2 jit_solution(1063346559495038192)
XLA Ops:
  0.0 0.8 slice_bitcast_fusion.1
  0.8 1.5 %fusion.coup = f32[16,16]{1,0:T(8,128)} fusion(s32[48]{0:T(128)S(1)} %get-tuple-element.6, f32[48]{0:T(128)} %param.13, s32[48]{0:T(128)S(1)} %get-tuple-element.5), kind=kOutput, calls=%fused_computation.1 | convolution fusion | flops 149760 | bytes 1600 | tf_op jit(solution)/shard_map/ka,kb->ab/dot_general | solution.py:417
  2.3 105.6 %hpsi.1 = f32[1,32,32,256]{3,2,1,0:T(8,128)} custom-call(f32[16,16]{1,0:T(8,128)} %fusion.coup, s32[32]{0:T(128)} %lt.1, s32[32]{0:T(128)} %rt.1, f32[1,32,256,256]{3,2,1,0:T(8,128)} %th_in.1, f32[2,1,256,256]{3,2,1,0:T(8,128)} %l_in.1, f32[2,1,256,256]{3,2,1,0:T(8,128)} %r_in.1), custom_call_target="tpu_custom_call" | custom-call | tf_op jit(solution)/shard_map/hpsi/pallas_call | solution.py:374
  107.8 2.3 %copy.9 = f32[1,32,32,256]{3,2,1,0:T(8,128)} copy(f32[1,32,32,256]{3,2,1,0:T(8,128)} %hpsi.1) | data formatting | bytes 2097152

commit v2 on v1

v2 whole, which is shorter than its diff:
```python
import functools

import jax
import jax.numpy as jnp
from jax import lax
from jax.experimental import pallas as pl
from jax.experimental.pallas import tpu as pltpu
from jax.sharding import PartitionSpec as P

MESH = pl.DeviceIdType.MESH
F32 = jnp.float32
BF16 = jnp.bfloat16
NX, NY, NZ = 4, 4, 8
MB = 256
SLAB = 32
DIST = (0, 1, 7, 2, 6, 3, 5, 4)
POS = tuple(DIST.index(d) for d in range(8))
GROUPS = (
    (0, 0), (0, 1), (1, 0), (3, 0), (1, 1), (3, 1), (2, 0), (2, 1),
    (2, 2), (1, 2), (3, 2), (2, 3), (1, 3), (3, 3), (0, 2), (0, 3),
)
TASKS = 2
NG = len(GROUPS)
PARTS = 4
PIECE = MB // PARTS


def pick(table, at):
    return sum((at == i).astype(jnp.int32) * v for i, v in enumerate(table) if v)


def split(v):
    hi = v.astype(BF16)
    return hi, (v - hi.astype(F32)).astype(BF16)


def dot(a, b):
    return jnp.dot(a, b, preferred_element_type=F32)


def kernel(
    pairs, coefs, lt, rt, th_in, l_in, r_in, o_ref,
    th, rin, rbuf, r3, lall, xbuf, x3, part, sib, f1, f2, fin,
    loc, own_s, l_s, l_r, z_s, z_r, t_s, t_r, ts_s, ts_r, q_s, q_r, x_s, x_r,
    p_s, p_r, f1_s, f1_r, f2_s, f2_r, o_s, o_r, o_l,
):
    row, blk = lax.axis_index("row"), lax.axis_index("blk")
    y, c = row // 2, row % 2
    x, z = blk // NZ, blk % NZ
    other = 1 - c

    def at(dx=0, dy=0, dz=0, flip=False):
        core = other if flip else c
        return (((y + dy) % NY) * 2 + core, ((x + dx) % NX) * NZ + (z + dz) % NZ)

    yp, ym, y2 = at(dy=1), at(dy=3), at(dy=2)
    xp, xm, x2 = at(dx=1), at(dx=3), at(dx=2)
    zp, zm = at(dz=1), at(dz=7)
    sb = at(flip=True)
    rp, rm, r2 = (row + 2) % 8, (row + 6) % 8, (row + 4) % 8
    srow = y * 2 + other
    sp, sm, s2 = (srow + 2) % 8, (srow + 6) % 8, (srow + 4) % 8

    def rc(src, dst, ss, rs, to):
        return pltpu.make_async_remote_copy(
            src_ref=src, dst_ref=dst, send_sem=ss, recv_sem=rs, device_id=to, device_id_type=MESH
        )

    sends = []
    mine = [2 * k + c for k in range(4)]
    theirs = [2 * k + other for k in range(4)]

    def view(of):
        return of[0].at[of[1]]

    def send(src, dst, ss, rs, to):
        rc(view(src), view(dst), view(ss), view(rs), to).start()
        sends.append((dst, ss))

    def got(dst, rs):
        rc(dst, dst, rs, rs, sb).wait_recv()

    def sent(src, ss):
        rc(src, src, ss, ss, sb).wait_send()

    H = MB // 2

    def piece(h):
        return l_in, (slice(None), 0, pl.ds(h * PIECE, PIECE))

    pltpu.make_async_copy(r_in.at[:, 0], rin, loc.at[0]).start()
    for h in range(PARTS):
        pltpu.make_async_copy(view(piece(h)), lall.at[h, row], loc.at[1 + h]).start()

    def own_theta(i):
        return pltpu.make_async_copy(
            th_in.at[0, x * NZ + (z + DIST[i]) % NZ], th.at[0, i], own_s.at[i]
        )

    barrier = pltpu.get_barrier_semaphore()
    partners = (yp, ym, xp, xm, x2, zp, zm, sb)
    for t in partners:
        pl.semaphore_signal(barrier, inc=1, device_id=t, device_id_type=MESH)
    pl.semaphore_wait(barrier, len(partners))

    def l_send(src, dst, h, i, to):
        send(src, (lall, dst), (l_s, (h, i)), (l_r, (h, i)), to)

    def l_own(h):
        for i, t in enumerate((yp, ym, sb)):
            l_send(piece(h), (h, row), h, i, t)

    def l_forward(h):
        for i, (r, t) in enumerate(((rm, yp), (rp, ym))):
            got(lall.at[h, r], l_r.at[h, i])
            l_send((lall, (h, r, i)), (h, r, i), h, 3 + i, t)
            l_send((lall, (h, r)), (h, r), h, 5 + i, sb)

    def l_rest(h):
        for i in range(2):
            got(lall.at[h, r2, i], l_r.at[h, 3 + i])
        l_send((lall, (h, r2)), (h, r2), h, 7, sb)
        got(lall.at[h, srow], l_r.at[h, 2])
        got(lall.at[h, sm], l_r.at[h, 5])
        got(lall.at[h, sp], l_r.at[h, 6])
        got(lall.at[h, s2], l_r.at[h, 7])
        pltpu.make_async_copy(view(piece(h)), lall.at[h, row], loc.at[1 + h]).wait()

    def theta_at(xx, i):
        return th_in, (0, xx * NZ + (z + i) % NZ)

    def send_theta(k):
        d = DIST[2 * k] + c * (DIST[2 * k + 1] - DIST[2 * k])
        send(theta_at((x + 1) % NX, d), (th, (3, mine[k])), (t_s, (0, k)), (t_r, (0, k)), xp)
        send(theta_at((x + 3) % NX, d), (th, (1, mine[k])), (t_s, (1, k)), (t_r, (1, k)), xm)

    def sib_theta(k):
        for s, dx in ((0, 3), (1, 1)):
            got(th.at[dx, mine[k]], t_r.at[s, k])
            send((th, (dx, mine[k])), (th, (dx, mine[k])), (ts_s, (s, k)), (ts_r, (s, k)), sb)

    def sib_theta_got(k):
        for s, dx in ((0, 3), (1, 1)):
            got(th.at[dx, theirs[k]], ts_r.at[s, k])

    def z_send(k, b, up):
        if up:
            src, dst = (rbuf, (POS[(8 - k) % 8], b)), (rbuf, (POS[(7 - k) % 8], b))
        else:
            src, dst = (rbuf, (POS[k], b)), (rbuf, (POS[k + 1], b))
        s = 0 if up else 1
        send(src, dst, (z_s, (s, k, b)), (z_r, (s, k, b)), zp if up else zm)

    def z_got(k, b, up):
        s = 0 if up else 1
        got(rbuf.at[POS[8 - k] if up else POS[k], b], z_r.at[s, k - 1, b])

    def zf(k, b):
        for up in (True, False):
            z_got(k, b, up)
            if k < 3 or b == (0 if up else 1):
                z_send(k, b, up)

    def z_forward(k):
        zf(k, 0)
        zf(k, 1)

    def split_r(pos):
        for b in range(2):
            hi, lo = split(rbuf[pos, b])
            r3[pos, b * MB : (b + 1) * MB, :] = hi
            r3[pos, (2 + b) * MB : (3 + b) * MB, :] = lo
            r3[pos, (4 + b) * MB : (5 + b) * MB, :] = hi

    def store_x(dx, b, first, rows, v):
        hi, lo = split(v)
        at = pl.ds(b * MB + first, rows)
        x3[dx, at, 0:MB] = hi
        x3[dx, at, MB : 2 * MB] = hi
        x3[dx, at, 2 * MB : 3 * MB] = lo

    def split_x(dx):
        for h in range(PARTS):
            for b in range(2):
                store_x(dx, b, h * PIECE, PIECE, xbuf[dx, h, b])

    def x_send(h):
        send((xbuf, (0, h)), (xbuf, (3, h)), (x_s, (0, h)), (x_r, (0, h)), xp)
        send((xbuf, (0, h)), (xbuf, (1, h)), (x_s, (1, h)), (x_r, (1, h)), xm)

    def x_forward(h):
        got(xbuf.at[3, h], x_r.at[0, h])
        send((xbuf, (3, h, 0)), (xbuf, (2, h, 0)), (x_s, (2, h)), (x_r, (2, h)), xp)
        got(xbuf.at[1, h], x_r.at[1, h])
        send((xbuf, (1, h, 1)), (xbuf, (2, h, 1)), (x_s, (3, h)), (x_r, (3, h)), xm)

    def x_rest(h):
        got(xbuf.at[2, h, 0], x_r.at[2, h])
        got(xbuf.at[2, h, 1], x_r.at[3, h])

    def q_first():
        d = pick(DIST, row)
        send(theta_at((x + 2) % NX, d), (th, (2, row)), (q_s, (8,)), (q_r, (8,)), x2)

    def q_own():
        got(th.at[2, row], q_r.at[8])
        for i, t in enumerate((yp, ym, sb)):
            send((th, (2, row)), (th, (2, row)), (q_s, (i,)), (q_r, (i,)), t)

    def q_forward():
        for i, (r, t) in enumerate(((rm, yp), (rp, ym))):
            got(th.at[2, r], q_r.at[i])
            rows = pl.ds(i * H, H)
            send((th, (2, r, rows)), (th, (2, r, rows)), (q_s, (3 + i,)), (q_r, (3 + i,)), t)
            send((th, (2, r)), (th, (2, r)), (q_s, (5 + i,)), (q_r, (5 + i,)), sb)

    def q_rest():
        for i in range(2):
            got(th.at[2, r2, pl.ds(i * H, H)], q_r.at[3 + i])
        send((th, (2, r2)), (th, (2, r2)), (q_s, (7,)), (q_r, (7,)), sb)
        got(th.at[2, srow], q_r.at[2])
        got(th.at[2, sm], q_r.at[5])
        got(th.at[2, sp], q_r.at[6])
        got(th.at[2, s2], q_r.at[7])

    row_ids = lax.broadcasted_iota(jnp.int32, (MB, MB), 0)
    col_ids = lax.broadcasted_iota(jnp.int32, (MB, MB), 1)
    rlim = (MB // 4) * rt[blk]

    def own_r():
        pltpu.make_async_copy(r_in.at[:, 0], rin, loc.at[0]).wait()
        for b in range(2):
            v = jnp.where((row_ids < rlim) & (col_ids < rlim), rin[b], 0.0)
            rbuf[0, b] = v.T
            z_send(0, b, True)
            z_send(0, b, False)
        for i in range(8):
            own_theta(i).start()

    bond = lax.broadcasted_iota(jnp.int32, (16, MB), 0)

    def couple(k, acc):
        here = bond == pairs[k, 0]
        return [
            acc[b] + jnp.where(here & (pairs[k, 1] == 2 * row + b), coefs[k], 0.0) for b in range(2)
        ]

    llim = (MB // 4) * lt[blk]
    strip = 32

    def dress(h):
        @pl.loop(0, PIECE // strip)
        def _(s):
            first = pl.multiple_of(s * strip, strip)
            rows = lax.broadcasted_iota(jnp.int32, (strip, MB), 0) + first + h * PIECE
            cols = lax.broadcasted_iota(jnp.int32, (strip, MB), 1)
            keep = (rows < llim) & (cols < llim)
            acc = [jnp.zeros((strip, MB), F32) for _ in range(2)]
            for a in range(16):
                v = lall[h, a // 2, a % 2, pl.ds(first, strip), :]
                for b in range(2):
                    acc[b] = acc[b] + coup[b][a : a + 1] * v
            for b in range(2):
                v = jnp.where(keep, acc[b], 0.0)
                xbuf[0, h, b, pl.ds(first, strip), :] = v
                store_x(0, b, first + h * PIECE, strip, v)

    def dress_send(h):
        l_rest(h)
        dress(h)
        x_send(h)

    l_own(0)
    l_own(1)
    q_first()
    send_theta(0)
    own_r()
    coup = lax.fori_loop(0, pairs.shape[0], couple, [jnp.zeros((16, MB), F32)] * 2)
    split_r(0)
    l_forward(0)
    l_own(2)
    l_forward(1)
    l_own(3)
    send_theta(1)
    l_forward(2)
    zf(1,0)
    dress_send(0)
    zf(1,1)
    dress_send(1)
    l_forward(3)
    dress_send(2)
    sib_theta(0)
    q_own()
    x_forward(0)
    dress_send(3)
    x_forward(1)
    split_r(1)
    send_theta(2)
    for i in range(8):
        own_theta(i).wait()

    def event1():
        split_r(2)
        x_forward(2)
        zf(2,0)
        zf(2,1)
        split_r(3)

    def event2():
        x_forward(3)
        split_x(1)
        sib_theta_got(0)

    def event3():
        split_x(3)
        q_forward()
        sib_theta(1)
        send_theta(3)

    def event4():
        sib_theta_got(1)

    def event5():
        zf(3,0)
        zf(3,1)

    def event6():
        for h in range(PARTS):
            x_rest(h)
        split_x(2)
        q_rest()

    def event7():
        sib_theta(2)

    def event8():
        split_r(4)
        split_r(5)

    def event9():
        sib_theta_got(2)

    def event10():
        sib_theta(3)

    def event11():
        z_got(4,0,True)
        z_got(4,1,False)
        split_r(6)
        split_r(7)

    def event12():
        sib_theta_got(3)

    events = {1: event1, 2: event2, 3: event3, 4: event4, 5: event5, 6: event6, 7: event7, 8: event8, 9: event9, 10: event10, 11: event11, 12: event12}

    def out_copy(g, j):
        dx, pair = pick([a for a, _ in GROUPS], g), pick([h for _, h in GROUPS], g)
        d = pick(DIST, pair * TASKS + j)
        q = x * NZ + (z + d) % NZ
        return dx, q

    yn, yd, yf = (y + 1) % NY, (y + 3) % NY, (y + 2) % NY

    def stage3(g):
        got(f2.at[g, 0], f2_r.at[g, 0])
        got(f2.at[g, 1], f2_r.at[g, 1])
        fin[g] = part[g, c, y] + f2[g, 0] + f2[g, 1]
        for j in range(TASKS):
            dx, q = out_copy(g, j)

            @pl.when(dx == 0)
            def _():
                pltpu.make_async_copy(fin.at[g, j], o_ref.at[0, q], o_l.at[g, j]).start()

            @pl.when(dx != 0)
            def _():
                to = (row, ((x + dx) % NX) * NZ + z)
                rc(fin.at[g, j], o_ref.at[0, q], o_s.at[g, j], o_r.at[g, j], to).start()

    def stage2(g):
        got(f1.at[g, 0], f1_r.at[g, 0])
        part[g, c, yn, 0] = part[g, c, yn, 0] + f1[g, 0]
        rc(part.at[g, c, yn], f2.at[g, 0], f2_s.at[g, 0], f2_r.at[g, 0], yp).start()
        got(f1.at[g, 1], f1_r.at[g, 1])
        part[g, c, yd, 1] = part[g, c, yd, 1] + f1[g, 1]
        rc(part.at[g, c, yd], f2.at[g, 1], f2_s.at[g, 1], f2_r.at[g, 1], ym).start()

    def stage1(g):
        got(sib.at[g], p_r.at[g])
        part[g, c, yf] = part[g, c, yf] + sib[g, yf]
        rc(part.at[g, c, yf, 0], f1.at[g, 0], f1_s.at[g, 0], f1_r.at[g, 0], yp).start()
        rc(part.at[g, c, yf, 1], f1.at[g, 1], f1_s.at[g, 1], f1_r.at[g, 1], ym).start()
        for yy in (yn, yd, y):
            part[g, c, yy] = part[g, c, yy] + sib[g, yy]

    def compute(g):
        dx, pair = pick([a for a, _ in GROUPS], g), pick([h for _, h in GROUPS], g)

        wides = []
        for j in range(TASKS):
            thi, tlo = split(th[dx, pair * TASKS + j])
            p = dot(x3[dx], jnp.concatenate([thi, tlo, thi], axis=0))
            phi, plo = split(jnp.concatenate([p[:MB], p[MB:]], axis=1))
            wides.append(jnp.concatenate([phi, phi, plo], axis=1))
        for j in range(TASKS):
            o = dot(wides[j], r3[pair * TASKS + j])
            for s in range(8):
                part[g, s % 2, s // 2, j] = o[s * SLAB : (s + 1) * SLAB, :]

        rc(part.at[g, other], sib.at[g], p_s.at[g], p_r.at[g], sb).start()

    @pl.loop(0, NG + 7)
    def _(g):
        @pl.when(g >= 7)
        def _():
            stage3(g - 7)

        @pl.when((g >= 4) & (g < NG + 4))
        def _():
            stage2(g - 4)

        @pl.when((g >= 2) & (g < NG + 2))
        def _():
            stage1(g - 2)

        for i, event in events.items():
            pl.when(g == i)(event)

        @pl.when(g < NG)
        def _():
            compute(g)

    @pl.loop(0, NG)
    def _(g):
        sent(part.at[g, other], p_s.at[g])
        sent(part.at[g, c, yf, 0], f1_s.at[g, 0])
        sent(part.at[g, c, yf, 1], f1_s.at[g, 1])
        sent(part.at[g, c, yn], f2_s.at[g, 0])
        sent(part.at[g, c, yd], f2_s.at[g, 1])
        for j in range(TASKS):
            dx, q = out_copy(g, j)
            back = ((x + NX - dx) % NX) * NZ + q % NZ

            @pl.when(dx == 0)
            def _():
                pltpu.make_async_copy(fin.at[g, j], o_ref.at[0, q], o_l.at[g, j]).wait()

            @pl.when(dx != 0)
            def _():
                sent(fin.at[g, j], o_s.at[g, j])
                got(o_ref.at[0, back], o_r.at[g, j])

    for like, ss in sends:
        sent(view(like), view(ss))


def apply(pairs, coefs, lt, rt, theta, left_env, right_env):
    dma = pltpu.SemaphoreType.DMA
    return pl.pallas_call(
        kernel,
        out_shape=jax.ShapeDtypeStruct((1, NX * NZ, SLAB, MB), F32),
        in_specs=[pl.BlockSpec(memory_space=pltpu.SMEM)] * 4 + [pl.BlockSpec(memory_space=pl.ANY)] * 3,
        out_specs=pl.BlockSpec(memory_space=pl.ANY),
        scratch_shapes=[
            pltpu.VMEM((4, 8, MB, MB), F32),
            pltpu.VMEM((2, MB, MB), F32),
            pltpu.VMEM((8, 2, MB, MB), F32),
            pltpu.VMEM((8, 6 * MB, MB), BF16),
            pltpu.VMEM((PARTS, 8, 2, PIECE, MB), F32),
            pltpu.VMEM((4, PARTS, 2, PIECE, MB), F32),
            pltpu.VMEM((4, 2 * MB, 3 * MB), BF16),
            pltpu.VMEM((NG, 2, 4, TASKS, SLAB, MB), F32),
            pltpu.VMEM((NG, 4, TASKS, SLAB, MB), F32),
            pltpu.VMEM((NG, 2, SLAB, MB), F32),
            pltpu.VMEM((NG, 2, TASKS, SLAB, MB), F32),
            pltpu.VMEM((NG, TASKS, SLAB, MB), F32),
            dma((1 + PARTS,)), dma((8,)),
            dma((PARTS, 8)), dma((PARTS, 8)),
            dma((2, 4, 2)), dma((2, 4, 2)),
            dma((2, 4)), dma((2, 4)),
            dma((2, 4)), dma((2, 4)),
            dma((9,)), dma((9,)),
            dma((4, PARTS)), dma((4, PARTS)),
            dma((NG,)), dma((NG,)),
            dma((NG, 2)), dma((NG, 2)),
            dma((NG, 2)), dma((NG, 2)),
            dma((NG, TASKS)), dma((NG, TASKS)), dma((NG, TASKS)),
        ],
        compiler_params=pltpu.CompilerParams(
            collective_id=0, has_side_effects=True, vmem_limit_bytes=56 * 2**20
        ),
        name="hpsi",
    )(pairs, coefs, lt, rt, theta, left_env, right_env)


def per_device(theta, left_env, right_env, left_tiles, right_tiles, pairs, coefs):
    return apply(pairs, coefs, left_tiles, right_tiles, theta, left_env, right_env)


def solution(mesh):
    return jax.shard_map(
        per_device,
        mesh=mesh,
        in_specs=(
            P("blk", None, None, None),
            P("row", "blk", None, None),
            P("row", "blk", None, None),
            P(),
            P(),
            P(),
            P(),
        ),
        out_specs=P("blk", None, "row", None),
        check_vma=False,
    )
```

time: 112 us -> 92.9 us (0.83)
  Pallas kernels: 106 us -> 88.2 us
  matrix products: 1.52 us -> 0 us
    pallas_call x1, Pallas kernels: 106 us -> 88.2 us  [apply(): pl.pallas_call(kernel, out_shape=jax.ShapeDtypeStruct((1, NX * NZ, SLAB,...]
    dot_general x1 -> x0, matrix products: 1.52 us -> none  [per_device(): jnp.einsum('ka,kb->ab', onehot_left * coefs[:, None], onehot_right, preci...]
    unnamed x1 -> x2, local copies, waits for them, and re-layouts: 2.31 us -> 3.68 us
where the time goes in v2:
time: 92.9 us; the launch traced here: 91.9 us
  Pallas kernels  88.2 us (95%)
  local copies, waits for them, and re-layouts  3.68 us (4%)
    pallas_call x1, Pallas kernels, apply(): pl.pallas_call(kernel, out_shape=jax.ShapeDtypeStruct((1, NX * NZ, SLAB,...  88.2 us
    unnamed x2, local copies, waits for them, and re-layouts  3.68 us

profile of v2, /device:TPU:1, one launch (start us, length us, event | category | flops | bytes accessed | tf_op | source)
XLA Modules:
  0.0 91.9 jit_solution(12847852944884213062)
XLA Ops:
  0.0 1.4 %copy.8.pairs = s32[48,2]{1,0:T(8,128)} copy(s32[48,2]{0,1:T(2,128)} %param.12) | data formatting | bytes 768 | tf_op args[5]
  1.4 88.2 %hpsi.1 = f32[1,32,32,256]{3,2,1,0:T(8,128)} custom-call(s32[48,2]{1,0:T(8,128)} %copy.8.pairs, f32[48]{0:T(128)} %coefs.1, s32[32]{0:T(128)} %lt.1, s32[32]{0:T(128)} %rt.1, f32[1,32,256,256]{3,2,1,0:T(8,128)} %th_in.1, f32[2,1,256,256]{3,2,1,0:T(8,128)} %l_in.1, f32[2,1,256,256]{3,2,1,0:T(8,128)} %r_in.1), custom_call_target="tpu_custom_call" | custom-call | tf_op jit(solution)/shard_map/hpsi/pallas_call | solution.py:460
  89.6 2.3 %copy.10 = f32[1,32,32,256]{3,2,1,0:T(8,128)} copy(f32[1,32,32,256]{3,2,1,0:T(8,128)} %hpsi.1) | data formatting | bytes 2097152

commit v3 on v2

--- a/solution.py
+++ b/solution.py
@@ -295,7 +295,6 @@
     dress_send(3)
     x_forward(1)
     split_r(1)
-    send_theta(2)
     for i in range(8):
         own_theta(i).wait()
 
@@ -308,6 +307,7 @@
 
     def event2():
         x_forward(3)
+        send_theta(2)
         split_x(1)
         sib_theta_got(0)
 

time: 92.9 us -> 92.7 us (level)
  no operation moved by 1% of the time
where the time goes in v3:
time: 92.7 us; the launch traced here: 92 us
  Pallas kernels  88.3 us (95%)
  local copies, waits for them, and re-layouts  3.68 us (4%)
    pallas_call x1, Pallas kernels, apply(): pl.pallas_call(kernel, out_shape=jax.ShapeDtypeStruct((1, NX * NZ, SLAB,...  88.3 us
    unnamed x2, local copies, waits for them, and re-layouts  3.68 us

profile of v3, /device:TPU:1, one launch (start us, length us, event | category | flops | bytes accessed | tf_op | source)
XLA Modules:
  0.0 92.0 jit_solution(16750779283668794694)
XLA Ops:
  0.0 1.4 %copy.8.pairs = s32[48,2]{1,0:T(8,128)} copy(s32[48,2]{0,1:T(2,128)} %param.12) | data formatting | bytes 768 | tf_op args[5]
  1.4 88.3 %hpsi.1 = f32[1,32,32,256]{3,2,1,0:T(8,128)} custom-call(s32[48,2]{1,0:T(8,128)} %copy.8.pairs, f32[48]{0:T(128)} %coefs.1, s32[32]{0:T(128)} %lt.1, s32[32]{0:T(128)} %rt.1, f32[1,32,256,256]{3,2,1,0:T(8,128)} %th_in.1, f32[2,1,256,256]{3,2,1,0:T(8,128)} %l_in.1, f32[2,1,256,256]{3,2,1,0:T(8,128)} %r_in.1), custom_call_target="tpu_custom_call" | custom-call | tf_op jit(solution)/shard_map/hpsi/pallas_call | solution.py:460
  89.7 2.3 %copy.10 = f32[1,32,32,256]{3,2,1,0:T(8,128)} copy(f32[1,32,32,256]{3,2,1,0:T(8,128)} %hpsi.1) | data formatting | bytes 2097152
